TPU v7x, 128 devices: a whole 4x4x4 slice. The times are simulated.
128 devices in a mesh: ctx: 32 (over y, x, core), head: 4 (over z).
Axes of the slice: x: 4, y: 4, z: 4, core: 2. Of those that a mesh axis runs over, the one named last changes fastest.
Arguments:
- queries: bfloat16 [65536, 2048], P('ctx', 'head'), may hold values from -6 to 6
- key_rows: bfloat16 [65536, 2048], P('ctx', 'head'), may hold values from -6 to 6
- value_rows: bfloat16 [65536, 2048], P('ctx', 'head'), may hold values from -6 to 6
- level_codes: int32 [65536, 21], P('ctx'), may hold values from 0 to 15
- level_coefs: float32 [16, 16], P('head'), may hold values from 0.1 to 1
- norm_gain: float32 [2048], P('head'), may hold values from 0.1 to 1.9
- w_query: bfloat16 [2048, 2048], replicated, may hold values from -1 to 1
- w_key: bfloat16 [2048, 512], replicated, may hold values from -1 to 1
- w_value: bfloat16 [2048, 512], replicated, may hold values from -0.125 to 0.125
- lookback: int32 [65536], P(('ctx', 'head')), may hold values from 0 to 256
Outputs:
- fenwick_out: bfloat16 [65536, 2048], P('ctx', 'head')
- attended: bfloat16 [65536, 2048], P(('ctx', 'head'))
All inputs are finite; a program needn't handle non-finite values.
Results may differ from a plain program's by a relative error of at most 0.014.
Values may be sent and summed in bfloat16 or wider, within the bound.
A program may use at most 192 MiB of HBM per device.

v0:
```python
import functools

import jax
import jax.numpy as jnp
from jax import lax
from jax.experimental import pallas as pl
from jax.experimental.pallas import tpu as pltpu
from jax.sharding import PartitionSpec as P

HD = 128
HEADS = 16
KV_HEADS = 4
GROUPS = HEADS // KV_HEADS
WIN = 256
NCOEF = 16
N_HEAD = 4
SIDE = 4
FAR = 5
HERE = HEADS // N_HEAD
CHUNK = 256
HALF = CHUNK // 2
ROWS = 128
NEAR_BITS = 8
MESH = pl.DeviceIdType.MESH
BF = jnp.bfloat16
F32 = jnp.float32
SCALE = HD ** (-0.5)
LOG2E = 1.4426950408889634


def mm(a, b):
    return jnp.dot(a, b, preferred_element_type=F32)


def mm_nt(a, b):
    return lax.dot_general(a, b, (((1,), (1,)), ((), ())), preferred_element_type=F32)


def body(
    q_hbm, k_hbm, v_hbm, codes_hbm, coef_hbm, gain_hbm, wq_hbm, wk_hbm, wv_hbm, look_hbm,
    fen_hbm, att_hbm,
    q_v, k_v, v_v, qt, vt, codes, coef, gain, gain_t, look, lam, lev, loc, cst, lst,
    tot, totb, crecv, xr, yr, far, fen, xg, w_v, qs, kvb, bias, att,
    in_sem, w_sem, out_sem, small_sem,
    core_ss, core_rs, x_ss, x_rs, y_ss, y_rs, f_ss, f_rs, z_ss, z_rs, h_ss, h_rs,
):
    tok = q_hbm.shape[0]
    chunks = tok // CHUNK
    seg = tok // N_HEAD
    d_model = wq_hbm.shape[0]
    kvd = wk_hbm.shape[1]
    feat = HERE * HD
    n_ctx = lax.axis_size("ctx")

    c = lax.axis_index("ctx")
    z = lax.axis_index("head")
    core = lax.rem(c, 2)
    cx = lax.rem(c // 2, SIDE)
    cy = c // (2 * SIDE)
    shard = c * N_HEAD + z

    def at_x(v):
        return (cy * 2 * SIDE + v * 2 + core, z)

    def at_y(v):
        return (v * 2 * SIDE + cx * 2 + core, z)

    def at_z(v):
        return (c, v)

    other_core = (c + 1 - 2 * core, z)
    nshard = n_ctx * N_HEAD
    nxt = lax.rem(shard + 1, nshard)
    prv = lax.rem(shard + nshard - 1, nshard)
    next_dev = (nxt // N_HEAD, lax.rem(nxt, N_HEAD))
    prev_dev = (prv // N_HEAD, lax.rem(prv, N_HEAD))

    half_tok = tok // 2
    first = []
    for n in range(2):
        rows = pl.ds(n * half_tok, half_tok)
        pair = []
        for a, (src, dst) in enumerate(((v_hbm, v_v), (k_hbm, k_v))):
            cp = pltpu.make_async_copy(src.at[rows], dst.at[rows], in_sem.at[n, a])
            cp.start()
            pair.append(cp)
        first.append(pair)
    small = []
    for a, (src, dst) in enumerate(
        ((codes_hbm, codes), (coef_hbm, coef), (gain_hbm, gain), (look_hbm, look))
    ):
        cp = pltpu.make_async_copy(src, dst, small_sem.at[a])
        cp.start()
        small.append(cp)
    q_in = pltpu.make_async_copy(q_hbm, q_v, in_sem.at[2, 0])
    q_in.start()
    w_in = [
        pltpu.make_async_copy(wk_hbm, w_v.at[:, pl.ds(d_model, kvd)], w_sem.at[0]),
        pltpu.make_async_copy(wv_hbm, w_v.at[:, pl.ds(d_model + kvd, kvd)], w_sem.at[1]),
        pltpu.make_async_copy(wq_hbm, w_v.at[:, pl.ds(0, d_model)], w_sem.at[2]),
    ]
    for cp in w_in:
        cp.start()

    barrier = pltpu.get_barrier_semaphore()
    friends = [other_core, next_dev, prev_dev]
    for s in range(1, SIDE):
        friends.append(at_x(lax.rem(cx + s, SIDE)))
        friends.append(at_y(lax.rem(cy + s, SIDE)))
        friends.append(at_z(lax.rem(z + s, N_HEAD)))
    for dev in friends:
        pl.semaphore_signal(barrier, inc=1, device_id=dev, device_id_type=MESH)

    for n in range(2):
        for cp in first[n]:
            cp.wait()

        def state_step(i, carry, n=n):
            start = pl.multiple_of(i * CHUNK, CHUNK)
            rows = pl.ds(start, CHUNK)
            vtc = v_v[rows, :].T
            vt[:, rows] = vtc
            for h in range(HERE):
                hs = slice(h * HD, (h + 1) * HD)
                cst[i, hs, :] = mm(vtc[hs, :], k_v[rows, hs])
            return carry

        lax.fori_loop(n * chunks // 2, (n + 1) * chunks // 2, state_step, 0)

    pairs = [cst[2 * j] + cst[2 * j + 1] for j in range(4)]
    lo4 = pairs[0] + pairs[1]
    total = lo4 + (pairs[2] + pairs[3])
    tot[...] = total
    totb[...] = total.astype(BF)
    for j in range(4):
        lst[j] = cst[2 * j].astype(BF)
    lst[4] = pairs[0].astype(BF)
    lst[5] = pairs[2].astype(BF)
    lst[6] = lo4.astype(BF)

    pl.semaphore_wait(barrier, len(friends))
    core_cp = pltpu.make_async_remote_copy(
        src_ref=totb, dst_ref=crecv, send_sem=core_ss.at[0], recv_sem=core_rs.at[0],
        device_id=other_core, device_id_type=MESH,
    )
    core_cp.start()

    for cp in small:
        cp.wait()
    si = lax.broadcasted_iota(jnp.int32, (HALF, HALF), 0)
    ti = lax.broadcasted_iota(jnp.int32, (HALF, HALF), 1)
    diff = jnp.bitwise_xor(si, ti)
    level = jnp.zeros((HALF, HALF), jnp.int32)
    for b in range(NEAR_BITS - 1):
        level = level + jnp.where(diff >= (1 << b), 1, 0)
    lev[...] = jnp.where(si <= ti, level, 99)
    for h in range(HERE):
        gain_t[h * HD : (h + 1) * HD, :] = jnp.broadcast_to(gain[h : h + 1, :], (HD, HD)).T

    my_half = pl.multiple_of(core * (feat // 2), feat // 2)
    half_rows = pl.ds(my_half, feat // 2)

    core_cp.wait_recv()
    xr[cx] = (tot[half_rows, :] + crecv[half_rows, :].astype(F32)).astype(BF)
    x_cps = []
    for s in (2, 1, 3):
        cp = pltpu.make_async_remote_copy(
            src_ref=xr.at[cx], dst_ref=xr.at[cx], send_sem=x_ss.at[s], recv_sem=x_rs.at[s],
            device_id=at_x(lax.rem(cx + s, SIDE)), device_id_type=MESH,
        )
        cp.start()
        x_cps.append(cp)
    far[:, 0:HD] = jnp.where(core == 1, crecv[...].astype(F32), 0.0).astype(BF)

    def lam_step(i, carry):
        cols = pl.ds(pl.multiple_of(i * CHUNK, CHUNK), CHUNK)
        cd = codes[:, cols]
        for h in range(HERE):
            acc = jnp.full(cd.shape, coef[h, 0], F32)
            for n in range(1, NCOEF):
                acc = jnp.where(cd == n, coef[h, n], acc)
            lam[h, :, cols] = acc
        return carry

    lax.fori_loop(0, chunks, lam_step, 0)
    q_in.wait()

    def q_step(i, carry):
        rows = pl.ds(pl.multiple_of(i * CHUNK, CHUNK), CHUNK)
        qt[:, rows] = q_v[rows, :].T
        return carry

    lax.fori_loop(0, chunks, q_step, 0)

    def local_chunk(i):
        t0 = i * CHUNK
        cols = slice(t0, t0 + CHUNK)

        def head(h, carry):
            hoff = pl.multiple_of(h * HD, HD)
            hrows = pl.ds(hoff, HD)
            qth = qt[hrows, cols]
            st = mm(k_v[cols, hrows], qth)
            lamh = lam.at[h]

            def quad(a):
                lo = t0 + a * HALF
                w = jnp.zeros((HALF, HALF), F32)
                lv = lev[...]
                for l in range(NEAR_BITS):
                    w = jnp.where(lv == l, lamh[l : l + 1, lo : lo + HALF], w)
                return (st[a * HALF : (a + 1) * HALF, a * HALF : (a + 1) * HALF] * w).astype(BF)

            cross = (
                st[:HALF, HALF:] * lamh[NEAR_BITS : NEAR_BITS + 1, t0 + HALF : t0 + CHUNK]
            ).astype(BF)
            top = jnp.concatenate([quad(0), cross], axis=1)
            low = jnp.concatenate([jnp.zeros((HALF, HALF), BF), quad(1)], axis=1)
            terms = jnp.concatenate([top, low], axis=0)
            acc = mm(vt[hrows, cols], terms)
            used = []
            if i & 1:
                used.append((i // 2, 9))
            if i & 2:
                used.append((4 + i // 4, 10))
            if i & 4:
                used.append((6, 11))
            for slot, l in used:
                ql = qth * jnp.broadcast_to(lamh[l : l + 1, cols], (HD, CHUNK)).astype(BF)
                acc = acc + mm(lst[slot, hrows, :], ql)
            loc[hrows, cols] = acc
            return carry

        lax.fori_loop(0, HERE, head, 0)

    for i in (7, 6):
        local_chunk(i)

    for cp in x_cps:
        cp.wait_recv()

    def m(cond):
        return jnp.where(cond, 1.0, 0.0).astype(F32)

    def level_pair(buf, pos):
        parts = [buf[j].astype(F32) for j in range(SIDE)]
        low = parts[0] + parts[1]
        one = parts[0] * m(pos == 1) + parts[2] * m(pos == 3)
        two = low * m(pos >= 2)
        return one.astype(BF), two.astype(BF), low + (parts[2] + parts[3])

    one, two, row_sum = level_pair(xr, cx)
    yr[cy] = row_sum.astype(BF)
    y_cps = []
    for s in (2, 1, 3):
        cp = pltpu.make_async_remote_copy(
            src_ref=yr.at[cy], dst_ref=yr.at[cy], send_sem=y_ss.at[s], recv_sem=y_rs.at[s],
            device_id=at_y(lax.rem(cy + s, SIDE)), device_id_type=MESH,
        )
        cp.start()
        y_cps.append(cp)
    far[half_rows, HD : 2 * HD] = one
    far[half_rows, 2 * HD : 3 * HD] = two

    def pass_on(n):
        piece = far.at[half_rows, pl.ds((2 * n + 1) * HD, 2 * HD)]
        cp = pltpu.make_async_remote_copy(
            src_ref=piece, dst_ref=piece, send_sem=f_ss.at[n], recv_sem=f_rs.at[n],
            device_id=other_core, device_id_type=MESH,
        )
        cp.start()
        return cp

    f_cps = [pass_on(0)]

    for i in (5, 4, 3, 2, 1, 0):
        local_chunk(i)

    ri = lax.broadcasted_iota(jnp.int32, (ROWS, WIN + ROWS), 0)
    ji = lax.broadcasted_iota(jnp.int32, (ROWS, WIN + ROWS), 1)
    gap = WIN + ri - ji
    for b in range(seg // ROWS):
        reach = jnp.broadcast_to(look[b : b + 1, :].astype(F32), (ROWS, ROWS)).T
        reach = jnp.concatenate([reach] * 3, axis=1).astype(jnp.int32)
        key_pos = shard * seg + b * ROWS - WIN + ji
        ok = (gap >= 0) & (gap <= reach) & (key_pos >= 0)
        bias[b] = jnp.where(ok, 0.0, -1e30)

    for cp in y_cps:
        cp.wait_recv()
    one, two, _ = level_pair(yr, cy)
    far[half_rows, 3 * HD : 4 * HD] = one
    far[half_rows, 4 * HD : 5 * HD] = two
    f_cps.append(pass_on(1))
    for cp in f_cps:
        cp.wait()

    def chunk_of(n):
        hf = 1 - n // N_HEAD
        j = lax.rem(n, N_HEAD)
        k = jnp.where(j == 0, 2, jnp.where(j == 1, 1, jnp.where(j == 2, 3, 0)))
        dest = lax.rem(z + k, N_HEAD)
        return hf, k, dest

    def z_copy(hf, k, dest):
        src_rows = pl.ds(pl.multiple_of(dest * seg + hf * CHUNK, CHUNK), CHUNK)
        return pltpu.make_async_remote_copy(
            src_ref=fen.at[src_rows],
            dst_ref=xg.at[
                pl.ds(pl.multiple_of(hf * CHUNK, CHUNK), CHUNK),
                pl.ds(pl.multiple_of(z * feat, feat), feat),
            ],
            send_sem=z_ss.at[hf, k],
            recv_sem=z_rs.at[hf, k],
            device_id=at_z(dest),
            device_id_type=MESH,
        )

    def far_step(n, carry):
        hf, k, dest = chunk_of(n)
        start = pl.multiple_of(dest * seg + hf * CHUNK, CHUNK)
        cols = pl.ds(start, CHUNK)
        for h in range(HERE):
            hs = slice(h * HD, (h + 1) * HD)
            qth = qt[hs, cols]
            parts = []
            for l in range(FAR):
                row = lam[h, 12 + l : 13 + l, cols]
                parts.append(qth * jnp.broadcast_to(row, (HD, CHUNK)).astype(BF))
            acc = loc[hs, cols] + mm(far[hs, :], jnp.concatenate(parts, axis=0))
            ms = jnp.sum(acc * acc, axis=0, keepdims=True)
            r = SCALE * lax.rsqrt(ms * (SCALE * SCALE / HD) + 1e-06)
            g = gain_t[hs, :]
            g = jnp.concatenate([g, g], axis=1)
            fen[cols, hs] = (acc * r * g).astype(BF).T

        @pl.when(k > 0)
        def _():
            z_copy(hf, k, dest).start()

        @pl.when(k == 0)
        def _():
            xg[
                pl.ds(pl.multiple_of(hf * CHUNK, CHUNK), CHUNK),
                pl.ds(pl.multiple_of(z * feat, feat), feat),
            ] = fen[cols, :]

        return carry

    lax.fori_loop(0, 2 * N_HEAD, far_step, 0)
    fen_out = pltpu.make_async_copy(fen, fen_hbm, out_sem.at[0])
    fen_out.start()
    for cp in w_in:
        cp.wait()

    def arrive(hf):
        for k in range(1, N_HEAD):
            z_copy(hf, k, lax.rem(z + k, N_HEAD)).wait_recv()

    def project(hf):
        rows = slice(hf * CHUNK, (hf + 1) * CHUNK)
        kv_rows = slice(WIN + hf * CHUNK, WIN + (hf + 1) * CHUNK)

        def kv_step(n, carry):
            off = pl.multiple_of(n * kvd, kvd)
            wcols = pl.ds(pl.multiple_of(d_model + n * kvd, kvd), kvd)
            kvb[kv_rows, pl.ds(off, kvd)] = mm(xg[rows, :], w_v[:, wcols]).astype(BF)
            return carry

        lax.fori_loop(0, 2, kv_step, 0)
        if hf == 1:
            halo.start()

        def q_proj(n, carry):
            off = pl.ds(pl.multiple_of(n * kvd, kvd), kvd)
            qs[rows, off] = mm(xg[rows, :], w_v[:, off]).astype(BF)
            return carry

        lax.fori_loop(0, d_model // kvd, q_proj, 0)

    halo = pltpu.make_async_remote_copy(
        src_ref=kvb.at[pl.ds(seg, WIN)], dst_ref=kvb.at[pl.ds(0, WIN)],
        send_sem=h_ss.at[0], recv_sem=h_rs.at[0], device_id=next_dev, device_id_type=MESH,
    )
    arrive(1)
    project(1)
    arrive(0)
    project(0)
    halo.wait_recv()

    ones = jnp.ones((WIN + ROWS, HD), BF)

    def att_step(n, carry):
        b = n // KV_HEADS
        g = lax.rem(n, KV_HEADS)
        rows = pl.ds(pl.multiple_of(b * ROWS, ROWS), ROWS)
        keys = pl.ds(pl.multiple_of(b * ROWS, ROWS), WIN + ROWS)
        kg = kvb[keys, pl.ds(pl.multiple_of(g * HD, HD), HD)]
        vg = kvb[keys, pl.ds(pl.multiple_of(kvd + g * HD, HD), HD)]
        va = jnp.concatenate([vg, ones], axis=1)
        mask = bias[b]
        for i in range(GROUPS):
            hcols = pl.ds(pl.multiple_of(g * GROUPS * HD + i * HD, HD), HD)
            s = mm_nt(qs[rows, hcols], kg) + mask
            top = jnp.max(s, axis=1, keepdims=True)
            p = jnp.exp2((s - top) * (SCALE * LOG2E)).astype(BF)
            o = mm(p, va)
            att[rows, hcols] = (o[:, :HD] / o[:, HD:]).astype(BF)
        return carry

    lax.fori_loop(0, seg // ROWS * KV_HEADS, att_step, 0)
    att_out = pltpu.make_async_copy(att, att_hbm, out_sem.at[1])
    att_out.start()

    core_cp.wait_send()
    for cp in x_cps + y_cps:
        cp.wait_send()
    for hf in range(2):
        for k in range(1, N_HEAD):
            z_copy(hf, k, lax.rem(z + k, N_HEAD)).wait_send()
    halo.wait_send()
    fen_out.wait()
    att_out.wait()


def shards(
    queries, key_rows, value_rows, level_codes, level_coefs, norm_gain, w_query, w_key, w_value,
    lookback,
):
    tok, feat = queries.shape
    levels = level_codes.shape[1]
    d_model = w_query.shape[0]
    kvd = w_key.shape[1]
    seg = tok // N_HEAD
    chunks = tok // CHUNK
    hbm = pl.BlockSpec(memory_space=pltpu.HBM)
    dma = pltpu.SemaphoreType.DMA
    return pl.pallas_call(
        body,
        out_shape=(
            jax.ShapeDtypeStruct((tok, feat), BF),
            jax.ShapeDtypeStruct((seg, d_model), BF),
        ),
        in_specs=[hbm] * 10,
        out_specs=(hbm, hbm),
        scratch_shapes=[
            pltpu.VMEM((tok, feat), BF),
            pltpu.VMEM((tok, feat), BF),
            pltpu.VMEM((tok, feat), BF),
            pltpu.VMEM((feat, tok), BF),
            pltpu.VMEM((feat, tok), BF),
            pltpu.VMEM((levels, tok), jnp.int32),
            pltpu.SMEM((HERE, NCOEF), F32),
            pltpu.VMEM((HERE, HD), F32),
            pltpu.VMEM((feat, HD), F32),
            pltpu.VMEM((seg // ROWS, ROWS), jnp.int32),
            pltpu.VMEM((HERE, levels, tok), F32),
            pltpu.VMEM((HALF, HALF), jnp.int32),
            pltpu.VMEM((feat, tok), F32),
            pltpu.VMEM((chunks, feat, HD), F32),
            pltpu.VMEM((7, feat, HD), BF),
            pltpu.VMEM((feat, HD), F32),
            pltpu.VMEM((feat, HD), BF),
            pltpu.VMEM((feat, HD), BF),
            pltpu.VMEM((SIDE, feat // 2, HD), BF),
            pltpu.VMEM((SIDE, feat // 2, HD), BF),
            pltpu.VMEM((feat, FAR * HD), BF),
            pltpu.VMEM((tok, feat), BF),
            pltpu.VMEM((seg, d_model), BF),
            pltpu.VMEM((d_model, d_model + 2 * kvd), BF),
            pltpu.VMEM((seg, d_model), BF),
            pltpu.VMEM((seg + WIN, 2 * kvd), BF),
            pltpu.VMEM((seg // ROWS, ROWS, WIN + ROWS), F32),
            pltpu.VMEM((seg, d_model), BF),
            dma((3, 2)), dma((3,)), dma((2,)), dma((4,)),
            dma((1,)), dma((1,)), dma((SIDE,)), dma((SIDE,)), dma((SIDE,)), dma((SIDE,)),
            dma((2,)), dma((2,)), dma((2, N_HEAD)), dma((2, N_HEAD)), dma((1,)), dma((1,)),
        ],
        compiler_params=pltpu.CompilerParams(
            collective_id=0, has_side_effects=True, vmem_limit_bytes=60 << 20
        ),
    )(
        queries, key_rows, value_rows, level_codes.T, level_coefs,
        norm_gain.reshape(HERE, HD), w_query, w_key, w_value, lookback.reshape(seg // ROWS, ROWS),
    )


def solution(mesh):
    in_specs = (
        P("ctx", "head"),
        P("ctx", "head"),
        P("ctx", "head"),
        P("ctx", None),
        P("head", None),
        P("head"),
        P(),
        P(),
        P(),
        P(("ctx", "head")),
    )
    out_specs = (P("ctx", "head"), P(("ctx", "head"), None))
    return jax.shard_map(shards, mesh=mesh, in_specs=in_specs, out_specs=out_specs, check_vma=False)
```

profile of v0, /device:TPU:1, one launch (start us, length us, event | category | flops | bytes accessed | tf_op | source)
XLA Modules:
  0.0 80.3 jit_solution(1357766559988819148)
XLA Ops:
  0.6 75.1 %shard_map.113 = (bf16[2048,512]{1,0:T(8,128)(2,1)}, bf16[512,2048]{1,0:T(8,128)(2,1)}) custom-call(bf16[2048,512]{1,0:T(8,128)(2,1)} %q_hbm.1, bf16[2048,512]{1,0:T(8,128)(2,1)} %k_hbm.1, bf16[2048,512]{1,0:T(8,128)(2,1)} %v_hbm.1, s32[21,2048]{1,0:T(8,128)} %bitcast.3, f32[4,16]{1,0:T(4,128)} %coef_hbm.1, f32[4,128]{1,0:T(4,128)} %bitcast.4, ...), custom_call_target="tpu_custom_call" | custom-call | tf_op jit(solution)/shard_map/pallas_call | solution.py:438
  75.8 0.0 copy-start
  75.8 3.2 %copy.14 = bf16[2048,512]{1,0:T(8,128)(2,1)} copy(bf16[2048,512]{1,0:T(8,128)(2,1)} %get-tuple-element.4) | data formatting | bytes 4194304
  79.0 0.0 copy-done
  79.0 1.3 %copy.15 = bf16[512,2048]{1,0:T(8,128)(2,1)} copy(bf16[512,2048]{1,0:T(8,128)(2,1)S(1)} %copy-done) | data formatting | bytes 4194304
Async XLA Ops:
  75.8 3.2 %copy-start = (bf16[512,2048]{1,0:T(8,128)(2,1)S(1)}, bf16[512,2048]{1,0:T(8,128)(2,1)}, u32[]{:S(2)}) copy-start(bf16[512,2048]{1,0:T(8,128)(2,1)} %get-tuple-element.5) | copy-start | bytes 6291460
where the time goes:
time: 80.4 us; the launch traced here: 80.3 us
  Pallas kernels  75.1 us (93%)
  local copies, waits for them, and re-layouts  4.52 us (6%)
    pallas_call x1, Pallas kernels, shards(): pl.pallas_call(body, out_shape=(jax.ShapeDtypeStruct((tok, feat), BF), ja...  75.1 us
    unnamed x4, local copies, waits for them, and re-layouts  4.52 us

commit v1 on v0

--- a/solution.py
+++ b/solution.py
@@ -25,6 +25,7 @@
 BF = jnp.bfloat16
 F32 = jnp.float32
 SCALE = HD ** (-0.5)
+THROTTLE = True
 LOG2E = 1.4426950408889634
 
 
@@ -40,9 +41,9 @@
     q_hbm, k_hbm, v_hbm, codes_hbm, coef_hbm, gain_hbm, wq_hbm, wk_hbm, wv_hbm, look_hbm,
     fen_hbm, att_hbm,
     q_v, k_v, v_v, qt, vt, codes, coef, gain, gain_t, look, lam, lev, loc, cst, lst,
-    tot, totb, crecv, xr, yr, far, fen, xg, w_v, qs, kvb, bias, att,
+    tot, totb, crecv, xr, yr, far, fen, xg, w_v, qs, kvb, bias, att, relay, part,
     in_sem, w_sem, out_sem, small_sem,
-    core_ss, core_rs, x_ss, x_rs, y_ss, y_rs, f_ss, f_rs, z_ss, z_rs, h_ss, h_rs,
+    core_ss, core_rs, x_ss, x_rs, y_ss, y_rs, f_ss, f_rs, z_ss, z_rs, h_ss, h_rs, r_ss, r_rs,
 ):
     tok = q_hbm.shape[0]
     chunks = tok // CHUNK
@@ -74,6 +75,15 @@
     prv = lax.rem(shard + nshard - 1, nshard)
     next_dev = (nxt // N_HEAD, lax.rem(nxt, N_HEAD))
     prev_dev = (prv // N_HEAD, lax.rem(prv, N_HEAD))
+
+    barrier = pltpu.get_barrier_semaphore()
+    friends = [other_core, next_dev, prev_dev]
+    for s in range(1, SIDE):
+        friends.append(at_x(lax.rem(cx + s, SIDE)))
+        friends.append(at_y(lax.rem(cy + s, SIDE)))
+        friends.append(at_z(lax.rem(z + s, N_HEAD)))
+    for dev in friends:
+        pl.semaphore_signal(barrier, inc=1, device_id=dev, device_id_type=MESH)
 
     half_tok = tok // 2
     first = []
@@ -102,15 +112,6 @@
     for cp in w_in:
         cp.start()
 
-    barrier = pltpu.get_barrier_semaphore()
-    friends = [other_core, next_dev, prev_dev]
-    for s in range(1, SIDE):
-        friends.append(at_x(lax.rem(cx + s, SIDE)))
-        friends.append(at_y(lax.rem(cy + s, SIDE)))
-        friends.append(at_z(lax.rem(z + s, N_HEAD)))
-    for dev in friends:
-        pl.semaphore_signal(barrier, inc=1, device_id=dev, device_id_type=MESH)
-
     for n in range(2):
         for cp in first[n]:
             cp.wait()
@@ -334,9 +335,9 @@
             g = jnp.concatenate([g, g], axis=1)
             fen[cols, hs] = (acc * r * g).astype(BF).T
 
-        @pl.when(k > 0)
+        @pl.when((k > 0) & (hf == 1))
         def _():
-            z_copy(hf, k, dest).start()
+            z_copy(1, k, dest).start()
 
         @pl.when(k == 0)
         def _():
@@ -347,80 +348,128 @@
 
         return carry
 
+    def to_z(k):
+        return lax.rem(z + k, N_HEAD)
+
     lax.fori_loop(0, 2 * N_HEAD, far_step, 0)
     fen_out = pltpu.make_async_copy(fen, fen_hbm, out_sem.at[0])
     fen_out.start()
-    for cp in w_in:
-        cp.wait()
-
-    def arrive(hf):
-        for k in range(1, N_HEAD):
-            z_copy(hf, k, lax.rem(z + k, N_HEAD)).wait_recv()
-
-    def project(hf):
-        rows = slice(hf * CHUNK, (hf + 1) * CHUNK)
-        kv_rows = slice(WIN + hf * CHUNK, WIN + (hf + 1) * CHUNK)
-
-        def kv_step(n, carry):
-            off = pl.multiple_of(n * kvd, kvd)
-            wcols = pl.ds(pl.multiple_of(d_model + n * kvd, kvd), kvd)
-            kvb[kv_rows, pl.ds(off, kvd)] = mm(xg[rows, :], w_v[:, wcols]).astype(BF)
-            return carry
-
-        lax.fori_loop(0, 2, kv_step, 0)
-        if hf == 1:
-            halo.start()
-
-        def q_proj(n, carry):
-            off = pl.ds(pl.multiple_of(n * kvd, kvd), kvd)
-            qs[rows, off] = mm(xg[rows, :], w_v[:, off]).astype(BF)
-            return carry
-
-        lax.fori_loop(0, d_model // kvd, q_proj, 0)
-
+
+    if THROTTLE:
+        for k in (1, 3, 2):
+            z_copy(1, k, to_z(k)).wait_send()
+    hop = pltpu.make_async_remote_copy(
+        src_ref=fen.at[pl.ds(pl.multiple_of(to_z(2) * seg, CHUNK), CHUNK)],
+        dst_ref=relay,
+        send_sem=r_ss.at[0], recv_sem=r_rs.at[0],
+        device_id=at_z(to_z(3)), device_id_type=MESH,
+    )
+    hop.start()
+    z_copy(0, 1, to_z(1)).start()
+    z_copy(0, 3, to_z(3)).start()
+    onward = pltpu.make_async_remote_copy(
+        src_ref=relay,
+        dst_ref=xg.at[pl.ds(0, CHUNK), pl.ds(pl.multiple_of(to_z(1) * feat, feat), feat)],
+        send_sem=z_ss.at[0, 2], recv_sem=z_rs.at[0, 2],
+        device_id=at_z(to_z(3)), device_id_type=MESH,
+    )
     halo = pltpu.make_async_remote_copy(
         src_ref=kvb.at[pl.ds(seg, WIN)], dst_ref=kvb.at[pl.ds(0, WIN)],
         send_sem=h_ss.at[0], recv_sem=h_rs.at[0], device_id=next_dev, device_id_type=MESH,
     )
-    arrive(1)
-    project(1)
-    arrive(0)
-    project(0)
-    halo.wait_recv()
+    for cp in w_in:
+        cp.wait()
+
+    for k in (1, 3, 2):
+        z_copy(1, k, to_z(k)).wait_recv()
+    late = slice(CHUNK, 2 * CHUNK)
+    for n in range(2):
+        wcols = slice(d_model + n * kvd, d_model + (n + 1) * kvd)
+        kvb[WIN + CHUNK :, n * kvd : (n + 1) * kvd] = mm(xg[late, :], w_v[:, wcols]).astype(BF)
+    halo.start()
+
+    def q_proj(n, carry):
+        off = pl.ds(pl.multiple_of(n * kvd, kvd), kvd)
+        qs[late, off] = mm(xg[late, :], w_v[:, off]).astype(BF)
+        return carry
+
+    lax.fori_loop(0, d_model // kvd, q_proj, 0)
+    hop.wait_recv()
+    onward.start()
+
+    def two(j, k, off):
+        total = None
+        for s in (j, k):
+            fs = pl.ds(pl.multiple_of(lax.rem(z + N_HEAD - s, N_HEAD) * feat, feat), feat)
+            term = mm(xg[0:CHUNK, fs], w_v[fs, off])
+            total = term if total is None else total + term
+        return total
+
+    z_copy(0, 1, to_z(1)).wait_recv()
+
+    def part_step(n, carry):
+        off = pl.ds(pl.multiple_of(n * kvd, kvd), kvd)
+        part[:, off] = two(0, 1, off)
+        return carry
+
+    lax.fori_loop(0, d_model // kvd + 2, part_step, 0)
+    z_copy(0, 3, to_z(3)).wait_recv()
+    onward.wait_recv()
+    for n in range(2):
+        wcols = pl.ds(d_model + n * kvd, kvd)
+        kvb[WIN : WIN + CHUNK, n * kvd : (n + 1) * kvd] = (part[:, wcols] + two(3, 2, wcols)).astype(BF)
+
+    def q_rest(n, carry):
+        off = pl.ds(pl.multiple_of(n * kvd, kvd), kvd)
+        qs[0:CHUNK, off] = (part[:, off] + two(3, 2, off)).astype(BF)
+        return carry
+
+    lax.fori_loop(0, d_model // kvd, q_rest, 0)
 
     ones = jnp.ones((WIN + ROWS, HD), BF)
 
-    def att_step(n, carry):
-        b = n // KV_HEADS
-        g = lax.rem(n, KV_HEADS)
-        rows = pl.ds(pl.multiple_of(b * ROWS, ROWS), ROWS)
-        keys = pl.ds(pl.multiple_of(b * ROWS, ROWS), WIN + ROWS)
-        kg = kvb[keys, pl.ds(pl.multiple_of(g * HD, HD), HD)]
-        vg = kvb[keys, pl.ds(pl.multiple_of(kvd + g * HD, HD), HD)]
+    def attend(b, g):
+        rows = slice(b * ROWS, (b + 1) * ROWS)
+        keys = slice(b * ROWS, b * ROWS + WIN + ROWS)
+        kg = kvb[keys, g * HD : (g + 1) * HD]
+        vg = kvb[keys, kvd + g * HD : kvd + (g + 1) * HD]
         va = jnp.concatenate([vg, ones], axis=1)
         mask = bias[b]
         for i in range(GROUPS):
-            hcols = pl.ds(pl.multiple_of(g * GROUPS * HD + i * HD, HD), HD)
+            hcols = slice((g * GROUPS + i) * HD, (g * GROUPS + i + 1) * HD)
             s = mm_nt(qs[rows, hcols], kg) + mask
             top = jnp.max(s, axis=1, keepdims=True)
             p = jnp.exp2((s - top) * (SCALE * LOG2E)).astype(BF)
             o = mm(p, va)
             att[rows, hcols] = (o[:, :HD] / o[:, HD:]).astype(BF)
-        return carry
-
-    lax.fori_loop(0, seg // ROWS * KV_HEADS, att_step, 0)
-    att_out = pltpu.make_async_copy(att, att_hbm, out_sem.at[1])
-    att_out.start()
+
+    def att_half(n):
+        for b in (2 * n, 2 * n + 1):
+            for g in range(KV_HEADS):
+                attend(b, g)
+        rows = pl.ds(n * CHUNK, CHUNK)
+        cp = pltpu.make_async_copy(att.at[rows], att_hbm.at[rows], out_sem.at[1 + n])
+        cp.start()
+        return cp
+
+    att_out = [att_half(1)]
+    halo.wait_recv()
+    att_out.append(att_half(0))
 
     core_cp.wait_send()
     for cp in x_cps + y_cps:
         cp.wait_send()
-    for hf in range(2):
-        for k in range(1, N_HEAD):
-            z_copy(hf, k, lax.rem(z + k, N_HEAD)).wait_send()
+    if not THROTTLE:
+        for k in (1, 3, 2):
+            z_copy(1, k, to_z(k)).wait_send()
+    z_copy(0, 1, to_z(1)).wait_send()
+    z_copy(0, 3, to_z(3)).wait_send()
+    hop.wait_send()
+    onward.wait_send()
     halo.wait_send()
     fen_out.wait()
-    att_out.wait()
+    for cp in att_out:
+        cp.wait()
 
 
 def shards(
@@ -472,9 +521,12 @@
             pltpu.VMEM((seg + WIN, 2 * kvd), BF),
             pltpu.VMEM((seg // ROWS, ROWS, WIN + ROWS), F32),
             pltpu.VMEM((seg, d_model), BF),
-            dma((3, 2)), dma((3,)), dma((2,)), dma((4,)),
+            pltpu.VMEM((CHUNK, feat), BF),
+            pltpu.VMEM((CHUNK, d_model + 2 * kvd), F32),
+            dma((3, 2)), dma((3,)), dma((3,)), dma((4,)),
             dma((1,)), dma((1,)), dma((SIDE,)), dma((SIDE,)), dma((SIDE,)), dma((SIDE,)),
             dma((2,)), dma((2,)), dma((2, N_HEAD)), dma((2, N_HEAD)), dma((1,)), dma((1,)),
+            dma((1,)), dma((1,)),
         ],
         compiler_params=pltpu.CompilerParams(
             collective_id=0, has_side_effects=True, vmem_limit_bytes=60 << 20

time: 80.4 us -> 70.4 us (0.88)
  Pallas kernels: 75.1 us -> 64.5 us
    pallas_call x1, Pallas kernels: 75.1 us -> 64.5 us  [shards(): pl.pallas_call(body, out_shape=(jax.ShapeDtypeStruct((tok, feat), BF), ja...]
where the time goes in v1:
time: 70.4 us; the launch traced here: 69.7 us
  Pallas kernels  64.5 us (92%)
  local copies, waits for them, and re-layouts  4.52 us (6%)
    pallas_call x1, Pallas kernels, shards(): pl.pallas_call(body, out_shape=(jax.ShapeDtypeStruct((tok, feat), BF), ja...  64.5 us
    unnamed x4, local copies, waits for them, and re-layouts  4.52 us

profile of v1, /device:TPU:1, one launch (start us, length us, event | category | flops | bytes accessed | tf_op | source)
XLA Modules:
  0.0 69.7 jit_solution(6998624762280286763)
XLA Ops:
  0.6 64.5 %shard_map.113 = (bf16[2048,512]{1,0:T(8,128)(2,1)}, bf16[512,2048]{1,0:T(8,128)(2,1)}) custom-call(bf16[2048,512]{1,0:T(8,128)(2,1)} %q_hbm.1, bf16[2048,512]{1,0:T(8,128)(2,1)} %k_hbm.1, bf16[2048,512]{1,0:T(8,128)(2,1)} %v_hbm.1, s32[21,2048]{1,0:T(8,128)} %bitcast.3, f32[4,16]{1,0:T(4,128)} %coef_hbm.1, f32[4,128]{1,0:T(4,128)} %bitcast.4, ...), custom_call_target="tpu_custom_call" | custom-call | tf_op jit(solution)/shard_map/pallas_call | solution.py:487
  65.2 0.0 copy-start
  65.2 3.2 %copy.14 = bf16[2048,512]{1,0:T(8,128)(2,1)} copy(bf16[2048,512]{1,0:T(8,128)(2,1)} %get-tuple-element.4) | data formatting | bytes 4194304
  68.4 0.0 copy-done
  68.4 1.3 %copy.15 = bf16[512,2048]{1,0:T(8,128)(2,1)} copy(bf16[512,2048]{1,0:T(8,128)(2,1)S(1)} %copy-done) | data formatting | bytes 4194304
Async XLA Ops:
  65.2 3.2 %copy-start = (bf16[512,2048]{1,0:T(8,128)(2,1)S(1)}, bf16[512,2048]{1,0:T(8,128)(2,1)}, u32[]{:S(2)}) copy-start(bf16[512,2048]{1,0:T(8,128)(2,1)} %get-tuple-element.5) | copy-start | bytes 6291460

commit v2 on v1

--- a/solution.py
+++ b/solution.py
@@ -39,10 +39,10 @@
 
 def body(
     q_hbm, k_hbm, v_hbm, codes_hbm, coef_hbm, gain_hbm, wq_hbm, wk_hbm, wv_hbm, look_hbm,
-    fen_hbm, att_hbm,
+    fen, qs, kvb, bias,
     q_v, k_v, v_v, qt, vt, codes, coef, gain, gain_t, look, lam, lev, loc, cst, lst,
-    tot, totb, crecv, xr, yr, far, fen, xg, w_v, qs, kvb, bias, att, relay, part,
-    in_sem, w_sem, out_sem, small_sem,
+    tot, totb, crecv, xr, yr, far, xg, w_v, relay, part,
+    in_sem, w_sem, small_sem,
     core_ss, core_rs, x_ss, x_rs, y_ss, y_rs, f_ss, f_rs, z_ss, z_rs, h_ss, h_rs, r_ss, r_rs,
 ):
     tok = q_hbm.shape[0]
@@ -85,10 +85,10 @@
     for dev in friends:
         pl.semaphore_signal(barrier, inc=1, device_id=dev, device_id_type=MESH)
 
-    half_tok = tok // 2
+    quarter = tok // 4
     first = []
-    for n in range(2):
-        rows = pl.ds(n * half_tok, half_tok)
+    for n in range(4):
+        rows = pl.ds(n * quarter, quarter)
         pair = []
         for a, (src, dst) in enumerate(((v_hbm, v_v), (k_hbm, k_v))):
             cp = pltpu.make_async_copy(src.at[rows], dst.at[rows], in_sem.at[n, a])
@@ -102,7 +102,7 @@
         cp = pltpu.make_async_copy(src, dst, small_sem.at[a])
         cp.start()
         small.append(cp)
-    q_in = pltpu.make_async_copy(q_hbm, q_v, in_sem.at[2, 0])
+    q_in = pltpu.make_async_copy(q_hbm, q_v, in_sem.at[4, 0])
     q_in.start()
     w_in = [
         pltpu.make_async_copy(wk_hbm, w_v.at[:, pl.ds(d_model, kvd)], w_sem.at[0]),
@@ -112,7 +112,7 @@
     for cp in w_in:
         cp.start()
 
-    for n in range(2):
+    for n in range(4):
         for cp in first[n]:
             cp.wait()
 
@@ -126,7 +126,7 @@
                 cst[i, hs, :] = mm(vtc[hs, :], k_v[rows, hs])
             return carry
 
-        lax.fori_loop(n * chunks // 2, (n + 1) * chunks // 2, state_step, 0)
+        lax.fori_loop(n * chunks // 4, (n + 1) * chunks // 4, state_step, 0)
 
     pairs = [cst[2 * j] + cst[2 * j + 1] for j in range(4)]
     lo4 = pairs[0] + pairs[1]
@@ -234,7 +234,7 @@
 
         lax.fori_loop(0, HERE, head, 0)
 
-    for i in (7, 6):
+    for i in (7, 5):
         local_chunk(i)
 
     for cp in x_cps:
@@ -274,18 +274,8 @@
 
     f_cps = [pass_on(0)]
 
-    for i in (5, 4, 3, 2, 1, 0):
+    for i in (3, 1):
         local_chunk(i)
-
-    ri = lax.broadcasted_iota(jnp.int32, (ROWS, WIN + ROWS), 0)
-    ji = lax.broadcasted_iota(jnp.int32, (ROWS, WIN + ROWS), 1)
-    gap = WIN + ri - ji
-    for b in range(seg // ROWS):
-        reach = jnp.broadcast_to(look[b : b + 1, :].astype(F32), (ROWS, ROWS)).T
-        reach = jnp.concatenate([reach] * 3, axis=1).astype(jnp.int32)
-        key_pos = shard * seg + b * ROWS - WIN + ji
-        ok = (gap >= 0) & (gap <= reach) & (key_pos >= 0)
-        bias[b] = jnp.where(ok, 0.0, -1e30)
 
     for cp in y_cps:
         cp.wait_recv()
@@ -351,9 +341,20 @@
     def to_z(k):
         return lax.rem(z + k, N_HEAD)
 
-    lax.fori_loop(0, 2 * N_HEAD, far_step, 0)
-    fen_out = pltpu.make_async_copy(fen, fen_hbm, out_sem.at[0])
-    fen_out.start()
+    lax.fori_loop(0, N_HEAD, far_step, 0)
+    for i in (6, 4, 2, 0):
+        local_chunk(i)
+    lax.fori_loop(N_HEAD, 2 * N_HEAD, far_step, 0)
+
+    ri = lax.broadcasted_iota(jnp.int32, (ROWS, WIN + ROWS), 0)
+    ji = lax.broadcasted_iota(jnp.int32, (ROWS, WIN + ROWS), 1)
+    gap = WIN + ri - ji
+    for b in range(seg // ROWS):
+        reach = jnp.broadcast_to(look[b : b + 1, :].astype(F32), (ROWS, ROWS)).T
+        reach = jnp.concatenate([reach] * 3, axis=1).astype(jnp.int32)
+        key_pos = shard * seg + b * ROWS - WIN + ji
+        ok = (gap >= 0) & (gap <= reach) & (key_pos >= 0)
+        bias[b] = jnp.where(ok, 0.0, -1e30)
 
     if THROTTLE:
         for k in (1, 3, 2):
@@ -426,6 +427,24 @@
 
     lax.fori_loop(0, d_model // kvd, q_rest, 0)
 
+    halo.wait_recv()
+    core_cp.wait_send()
+    for cp in x_cps + y_cps:
+        cp.wait_send()
+    if not THROTTLE:
+        for k in (1, 3, 2):
+            z_copy(1, k, to_z(k)).wait_send()
+    z_copy(0, 1, to_z(1)).wait_send()
+    z_copy(0, 3, to_z(3)).wait_send()
+    hop.wait_send()
+    onward.wait_send()
+    halo.wait_send()
+
+
+def attention(fen, qs, kvb, bias, fen_hbm, att_hbm, att, out_sem):
+    kvd = kvb.shape[1] // 2
+    fen_out = pltpu.make_async_copy(fen, fen_hbm, out_sem.at[0])
+    fen_out.start()
     ones = jnp.ones((WIN + ROWS, HD), BF)
 
     def attend(b, g):
@@ -443,32 +462,15 @@
             o = mm(p, va)
             att[rows, hcols] = (o[:, :HD] / o[:, HD:]).astype(BF)
 
-    def att_half(n):
-        for b in (2 * n, 2 * n + 1):
-            for g in range(KV_HEADS):
-                attend(b, g)
-        rows = pl.ds(n * CHUNK, CHUNK)
-        cp = pltpu.make_async_copy(att.at[rows], att_hbm.at[rows], out_sem.at[1 + n])
+    copies = [fen_out]
+    for b in range(qs.shape[0] // ROWS):
+        for g in range(KV_HEADS):
+            attend(b, g)
+        rows = pl.ds(b * ROWS, ROWS)
+        cp = pltpu.make_async_copy(att.at[rows], att_hbm.at[rows], out_sem.at[1 + b])
         cp.start()
-        return cp
-
-    att_out = [att_half(1)]
-    halo.wait_recv()
-    att_out.append(att_half(0))
-
-    core_cp.wait_send()
-    for cp in x_cps + y_cps:
-        cp.wait_send()
-    if not THROTTLE:
-        for k in (1, 3, 2):
-            z_copy(1, k, to_z(k)).wait_send()
-    z_copy(0, 1, to_z(1)).wait_send()
-    z_copy(0, 3, to_z(3)).wait_send()
-    hop.wait_send()
-    onward.wait_send()
-    halo.wait_send()
-    fen_out.wait()
-    for cp in att_out:
+        copies.append(cp)
+    for cp in copies:
         cp.wait()
 
 
@@ -483,15 +485,18 @@
     seg = tok // N_HEAD
     chunks = tok // CHUNK
     hbm = pl.BlockSpec(memory_space=pltpu.HBM)
+    vmem = pl.BlockSpec(memory_space=pltpu.VMEM)
     dma = pltpu.SemaphoreType.DMA
-    return pl.pallas_call(
+    mid = pl.pallas_call(
         body,
         out_shape=(
-            jax.ShapeDtypeStruct((tok, feat), BF),
-            jax.ShapeDtypeStruct((seg, d_model), BF),
+            pltpu.VMEM((tok, feat), BF),
+            pltpu.VMEM((seg, d_model), BF),
+            pltpu.VMEM((seg + WIN, 2 * kvd), BF),
+            pltpu.VMEM((seg // ROWS, ROWS, WIN + ROWS), F32),
         ),
         in_specs=[hbm] * 10,
-        out_specs=(hbm, hbm),
+        out_specs=(vmem,) * 4,
         scratch_shapes=[
             pltpu.VMEM((tok, feat), BF),
             pltpu.VMEM((tok, feat), BF),
@@ -514,27 +519,33 @@
             pltpu.VMEM((SIDE, feat // 2, HD), BF),
             pltpu.VMEM((SIDE, feat // 2, HD), BF),
             pltpu.VMEM((feat, FAR * HD), BF),
-            pltpu.VMEM((tok, feat), BF),
             pltpu.VMEM((seg, d_model), BF),
             pltpu.VMEM((d_model, d_model + 2 * kvd), BF),
-            pltpu.VMEM((seg, d_model), BF),
-            pltpu.VMEM((seg + WIN, 2 * kvd), BF),
-            pltpu.VMEM((seg // ROWS, ROWS, WIN + ROWS), F32),
-            pltpu.VMEM((seg, d_model), BF),
             pltpu.VMEM((CHUNK, feat), BF),
             pltpu.VMEM((CHUNK, d_model + 2 * kvd), F32),
-            dma((3, 2)), dma((3,)), dma((3,)), dma((4,)),
+            dma((5, 2)), dma((3,)), dma((4,)),
             dma((1,)), dma((1,)), dma((SIDE,)), dma((SIDE,)), dma((SIDE,)), dma((SIDE,)),
             dma((2,)), dma((2,)), dma((2, N_HEAD)), dma((2, N_HEAD)), dma((1,)), dma((1,)),
             dma((1,)), dma((1,)),
         ],
         compiler_params=pltpu.CompilerParams(
-            collective_id=0, has_side_effects=True, vmem_limit_bytes=60 << 20
+            collective_id=0, has_side_effects=True, vmem_limit_bytes=50 << 20
         ),
     )(
         queries, key_rows, value_rows, level_codes.T, level_coefs,
         norm_gain.reshape(HERE, HD), w_query, w_key, w_value, lookback.reshape(seg // ROWS, ROWS),
     )
+    return pl.pallas_call(
+        attention,
+        out_shape=(
+            jax.ShapeDtypeStruct((tok, feat), BF),
+            jax.ShapeDtypeStruct((seg, d_model), BF),
+        ),
+        in_specs=[vmem] * 4,
+        out_specs=(hbm, hbm),
+        scratch_shapes=[pltpu.VMEM((seg, d_model), BF), dma((1 + seg // ROWS,))],
+        compiler_params=pltpu.CompilerParams(vmem_limit_bytes=32 << 20),
+    )(*mid)
 
 
 def solution(mesh):

time: 70.4 us -> 62.4 us (0.89)
  local copies, waits for them, and re-layouts: 4.52 us -> 0 us
  Pallas kernels: 64.5 us -> 61.4 us
    unnamed x4 -> x0, local copies, waits for them, and re-layouts: 4.52 us -> none
    pallas_call x1 -> x2, Pallas kernels: 64.5 us -> 61.4 us  [the longest x1 55.4 us: shards(): pl.pallas_call(body, out_shape=(pltpu.VMEM((tok, feat), BF), pltpu.VMEM((...]
where the time goes in v2:
time: 62.4 us; the launch traced here: 62 us
  Pallas kernels  61.4 us (98%)
  between operations  0.64 us (1%)
    pallas_call x1, Pallas kernels, shards(): pl.pallas_call(body, out_shape=(pltpu.VMEM((tok, feat), BF), pltpu.VMEM((...  55.4 us
    pallas_call x1, Pallas kernels, shards(): pl.pallas_call(attention, out_shape=(jax.ShapeDtypeStruct((tok, feat), BF...  6.01 us

profile of v2, /device:TPU:1, one launch (start us, length us, event | category | flops | bytes accessed | tf_op | source)
XLA Modules:
  0.0 62.0 jit_solution(14403946062964642821)
XLA Ops:
  0.6 55.4 %shard_map.113 = (bf16[2048,512]{1,0:T(8,128)(2,1)S(1)}, bf16[512,2048]{1,0:T(8,128)(2,1)S(1)}, bf16[768,1024]{1,0:T(8,128)(2,1)S(1)}, f32[4,128,384]{2,1,0:T(8,128)S(1)}) custom-call(bf16[2048,512]{1,0:T(8,128)(2,1)} %q_hbm.1, bf16[2048,512]{1,0:T(8,128)(2,1)} %k_hbm.1, bf16[2048,512]{1,0:T(8,128)(2,1)} %v_hbm.1, s32[21,2048]{1,0:T(8,128)} %bitcast.3, ...), custom_call_target="tpu_custom_call" | custom-call | tf_op jit(solution)/shard_map/pallas_call | solution.py:490
  56.0 6.0 %shard_map.114 = (bf16[2048,512]{1,0:T(8,128)(2,1)}, bf16[512,2048]{1,0:T(8,128)(2,1)}) custom-call(bf16[2048,512]{1,0:T(8,128)(2,1)S(1)} %get-tuple-element.6.fen, bf16[512,2048]{1,0:T(8,128)(2,1)S(1)} %get-tuple-element.7.qs, bf16[768,1024]{1,0:T(8,128)(2,1)S(1)} %get-tuple-element.8.kvb, f32[4,128,384]{2,1,0:T(8,128)S(1)} %get-tuple-element.9.bias), custom_call_target="tpu_custom_call" | custom-call | tf_op jit(solution)/shard_map/pallas_call | solution.py:538

commit v3 on v2

--- a/solution.py
+++ b/solution.py
@@ -25,7 +25,7 @@
 BF = jnp.bfloat16
 F32 = jnp.float32
 SCALE = HD ** (-0.5)
-THROTTLE = True
+PLAN = ((7,), (5,), (3,), (1,), (6, 4, 2, 0))
 LOG2E = 1.4426950408889634
 
 
@@ -104,6 +104,69 @@
         small.append(cp)
     q_in = pltpu.make_async_copy(q_hbm, q_v, in_sem.at[4, 0])
     q_in.start()
+    def pair_states(b):
+        for n in range(4):
+            if b == 0:
+                for cp in first[n]:
+                    cp.wait()
+
+            def state_step(i, carry):
+                rows = pl.ds(pl.multiple_of(i * CHUNK, CHUNK), CHUNK)
+                for h in (2 * b, 2 * b + 1):
+                    hs = slice(h * HD, (h + 1) * HD)
+                    vtc = v_v[rows, hs].T
+                    vt[hs, rows] = vtc
+                    cst[i, hs, :] = mm(vtc, k_v[rows, hs])
+                return carry
+
+            lax.fori_loop(n * chunks // 4, (n + 1) * chunks // 4, state_step, 0)
+        hs = slice(2 * b * HD, (2 * b + 2) * HD)
+        pairs = [cst[2 * j, hs, :] + cst[2 * j + 1, hs, :] for j in range(4)]
+        lo4 = pairs[0] + pairs[1]
+        total = lo4 + (pairs[2] + pairs[3])
+        tot[hs, :] = total
+        totb[hs, :] = total.astype(BF)
+        for j in range(4):
+            lst[j, hs, :] = cst[2 * j, hs, :].astype(BF)
+        lst[4, hs, :] = pairs[0].astype(BF)
+        lst[5, hs, :] = pairs[2].astype(BF)
+        lst[6, hs, :] = lo4.astype(BF)
+
+    def core_copy(b):
+        hs = pl.ds(2 * b * HD, 2 * HD)
+        return pltpu.make_async_remote_copy(
+            src_ref=totb.at[hs], dst_ref=crecv.at[hs], send_sem=core_ss.at[b], recv_sem=core_rs.at[b],
+            device_id=other_core, device_id_type=MESH,
+        )
+
+    def mine(b):
+        return pl.ds(pl.multiple_of((2 * b + core) * HD, HD), HD)
+
+    def spread(buf, b, own, place, sends, recvs):
+        out = []
+        for s in (2, 1, 3):
+            cp = pltpu.make_async_remote_copy(
+                src_ref=buf.at[b, own], dst_ref=buf.at[b, own],
+                send_sem=sends.at[b, s], recv_sem=recvs.at[b, s],
+                device_id=place(lax.rem(own + s, SIDE)), device_id_type=MESH,
+            )
+            cp.start()
+            out.append(cp)
+        return out
+
+    def chip_sum(b):
+        core_cps[b].wait_recv()
+        rows = mine(b)
+        xr[b, cx] = (tot[rows, :] + crecv[rows, :].astype(F32)).astype(BF)
+        return spread(xr, b, cx, at_x, x_ss, x_rs)
+
+    pair_states(0)
+    pl.semaphore_wait(barrier, len(friends))
+    core_cps = [core_copy(0), core_copy(1)]
+    core_cps[0].start()
+    pair_states(1)
+    core_cps[1].start()
+    x_cps = [chip_sum(0)]
     w_in = [
         pltpu.make_async_copy(wk_hbm, w_v.at[:, pl.ds(d_model, kvd)], w_sem.at[0]),
         pltpu.make_async_copy(wv_hbm, w_v.at[:, pl.ds(d_model + kvd, kvd)], w_sem.at[1]),
@@ -111,40 +174,6 @@
     ]
     for cp in w_in:
         cp.start()
-
-    for n in range(4):
-        for cp in first[n]:
-            cp.wait()
-
-        def state_step(i, carry, n=n):
-            start = pl.multiple_of(i * CHUNK, CHUNK)
-            rows = pl.ds(start, CHUNK)
-            vtc = v_v[rows, :].T
-            vt[:, rows] = vtc
-            for h in range(HERE):
-                hs = slice(h * HD, (h + 1) * HD)
-                cst[i, hs, :] = mm(vtc[hs, :], k_v[rows, hs])
-            return carry
-
-        lax.fori_loop(n * chunks // 4, (n + 1) * chunks // 4, state_step, 0)
-
-    pairs = [cst[2 * j] + cst[2 * j + 1] for j in range(4)]
-    lo4 = pairs[0] + pairs[1]
-    total = lo4 + (pairs[2] + pairs[3])
-    tot[...] = total
-    totb[...] = total.astype(BF)
-    for j in range(4):
-        lst[j] = cst[2 * j].astype(BF)
-    lst[4] = pairs[0].astype(BF)
-    lst[5] = pairs[2].astype(BF)
-    lst[6] = lo4.astype(BF)
-
-    pl.semaphore_wait(barrier, len(friends))
-    core_cp = pltpu.make_async_remote_copy(
-        src_ref=totb, dst_ref=crecv, send_sem=core_ss.at[0], recv_sem=core_rs.at[0],
-        device_id=other_core, device_id_type=MESH,
-    )
-    core_cp.start()
 
     for cp in small:
         cp.wait()
@@ -158,19 +187,7 @@
     for h in range(HERE):
         gain_t[h * HD : (h + 1) * HD, :] = jnp.broadcast_to(gain[h : h + 1, :], (HD, HD)).T
 
-    my_half = pl.multiple_of(core * (feat // 2), feat // 2)
-    half_rows = pl.ds(my_half, feat // 2)
-
-    core_cp.wait_recv()
-    xr[cx] = (tot[half_rows, :] + crecv[half_rows, :].astype(F32)).astype(BF)
-    x_cps = []
-    for s in (2, 1, 3):
-        cp = pltpu.make_async_remote_copy(
-            src_ref=xr.at[cx], dst_ref=xr.at[cx], send_sem=x_ss.at[s], recv_sem=x_rs.at[s],
-            device_id=at_x(lax.rem(cx + s, SIDE)), device_id_type=MESH,
-        )
-        cp.start()
-        x_cps.append(cp)
+    x_cps.append(chip_sum(1))
     far[:, 0:HD] = jnp.where(core == 1, crecv[...].astype(F32), 0.0).astype(BF)
 
     def lam_step(i, carry):
@@ -232,86 +249,72 @@
             loc[hrows, cols] = acc
             return carry
 
-        lax.fori_loop(0, HERE, head, 0)
-
-    for i in (7, 5):
-        local_chunk(i)
-
-    for cp in x_cps:
-        cp.wait_recv()
+        lax.fori_loop(0, HERE, head, 0, unroll=2)
 
     def m(cond):
         return jnp.where(cond, 1.0, 0.0).astype(F32)
 
-    def level_pair(buf, pos):
-        parts = [buf[j].astype(F32) for j in range(SIDE)]
+    def level_pair(buf, b, pos, n, cps):
+        for cp in cps:
+            cp.wait_recv()
+        parts = [buf[b, j].astype(F32) for j in range(SIDE)]
         low = parts[0] + parts[1]
         one = parts[0] * m(pos == 1) + parts[2] * m(pos == 3)
         two = low * m(pos >= 2)
-        return one.astype(BF), two.astype(BF), low + (parts[2] + parts[3])
-
-    one, two, row_sum = level_pair(xr, cx)
-    yr[cy] = row_sum.astype(BF)
-    y_cps = []
-    for s in (2, 1, 3):
+        if n == 0:
+            yr[b, cy] = (low + (parts[2] + parts[3])).astype(BF)
+            y_cps.append(spread(yr, b, cy, at_y, y_ss, y_rs))
+        rows = mine(b)
+        far[rows, (2 * n + 1) * HD : (2 * n + 2) * HD] = one.astype(BF)
+        far[rows, (2 * n + 2) * HD : (2 * n + 3) * HD] = two.astype(BF)
+        piece = far.at[rows, pl.ds((2 * n + 1) * HD, 2 * HD)]
         cp = pltpu.make_async_remote_copy(
-            src_ref=yr.at[cy], dst_ref=yr.at[cy], send_sem=y_ss.at[s], recv_sem=y_rs.at[s],
-            device_id=at_y(lax.rem(cy + s, SIDE)), device_id_type=MESH,
-        )
-        cp.start()
-        y_cps.append(cp)
-    far[half_rows, HD : 2 * HD] = one
-    far[half_rows, 2 * HD : 3 * HD] = two
-
-    def pass_on(n):
-        piece = far.at[half_rows, pl.ds((2 * n + 1) * HD, 2 * HD)]
-        cp = pltpu.make_async_remote_copy(
-            src_ref=piece, dst_ref=piece, send_sem=f_ss.at[n], recv_sem=f_rs.at[n],
+            src_ref=piece, dst_ref=piece, send_sem=f_ss.at[n, b], recv_sem=f_rs.at[n, b],
             device_id=other_core, device_id_type=MESH,
         )
         cp.start()
-        return cp
-
-    f_cps = [pass_on(0)]
-
-    for i in (3, 1):
+        f_cps[b].append(cp)
+
+    y_cps = []
+    f_cps = [[], []]
+    for i in PLAN[0]:
         local_chunk(i)
-
-    for cp in y_cps:
-        cp.wait_recv()
-    one, two, _ = level_pair(yr, cy)
-    far[half_rows, 3 * HD : 4 * HD] = one
-    far[half_rows, 4 * HD : 5 * HD] = two
-    f_cps.append(pass_on(1))
-    for cp in f_cps:
-        cp.wait()
-
-    def chunk_of(n):
-        hf = 1 - n // N_HEAD
-        j = lax.rem(n, N_HEAD)
-        k = jnp.where(j == 0, 2, jnp.where(j == 1, 1, jnp.where(j == 2, 3, 0)))
-        dest = lax.rem(z + k, N_HEAD)
-        return hf, k, dest
-
-    def z_copy(hf, k, dest):
-        src_rows = pl.ds(pl.multiple_of(dest * seg + hf * CHUNK, CHUNK), CHUNK)
+    level_pair(xr, 0, cx, 0, x_cps[0])
+    for i in PLAN[1]:
+        local_chunk(i)
+    level_pair(xr, 1, cx, 0, x_cps[1])
+    for i in PLAN[2]:
+        local_chunk(i)
+    level_pair(yr, 0, cy, 1, y_cps[0])
+    for i in PLAN[3]:
+        local_chunk(i)
+
+    def to_z(k):
+        return lax.rem(z + k, N_HEAD)
+
+    def z_copy(hf, k, b):
+        dest = to_z(k)
+        width = feat if b is None else feat // 2
+        first_col = 0 if b is None else b * (feat // 2)
+        slot = hf if b is None else 1 + b
         return pltpu.make_async_remote_copy(
-            src_ref=fen.at[src_rows],
+            src_ref=fen.at[
+                pl.ds(pl.multiple_of(dest * seg + hf * CHUNK, CHUNK), CHUNK), pl.ds(first_col, width)
+            ],
             dst_ref=xg.at[
-                pl.ds(pl.multiple_of(hf * CHUNK, CHUNK), CHUNK),
-                pl.ds(pl.multiple_of(z * feat, feat), feat),
+                pl.ds(hf * CHUNK, CHUNK),
+                pl.ds(pl.multiple_of(z * feat + first_col, feat // 2), width),
             ],
-            send_sem=z_ss.at[hf, k],
-            recv_sem=z_rs.at[hf, k],
+            send_sem=z_ss.at[slot, k],
+            recv_sem=z_rs.at[slot, k],
             device_id=at_z(dest),
             device_id_type=MESH,
         )
 
-    def far_step(n, carry):
-        hf, k, dest = chunk_of(n)
-        start = pl.multiple_of(dest * seg + hf * CHUNK, CHUNK)
-        cols = pl.ds(start, CHUNK)
-        for h in range(HERE):
+    def far_step(n, hf, b):
+        k = jnp.where(n == 0, 2, jnp.where(n == 1, 1, jnp.where(n == 2, 3, 0)))
+        cols = pl.ds(pl.multiple_of(to_z(k) * seg + hf * CHUNK, CHUNK), CHUNK)
+        for h in range(HERE) if b is None else (2 * b, 2 * b + 1):
             hs = slice(h * HD, (h + 1) * HD)
             qth = qt[hs, cols]
             parts = []
@@ -325,40 +328,37 @@
             g = jnp.concatenate([g, g], axis=1)
             fen[cols, hs] = (acc * r * g).astype(BF).T
 
-        @pl.when((k > 0) & (hf == 1))
-        def _():
-            z_copy(1, k, dest).start()
-
-        @pl.when(k == 0)
+        if hf == 1:
+
+            @pl.when(k > 0)
+            def _():
+                z_copy(1, k, b).start()
+
+        @pl.when((k == 0) & (b != 0))
         def _():
             xg[
-                pl.ds(pl.multiple_of(hf * CHUNK, CHUNK), CHUNK),
+                pl.ds(hf * CHUNK, CHUNK),
                 pl.ds(pl.multiple_of(z * feat, feat), feat),
             ] = fen[cols, :]
 
-        return carry
-
-    def to_z(k):
-        return lax.rem(z + k, N_HEAD)
-
-    lax.fori_loop(0, N_HEAD, far_step, 0)
-    for i in (6, 4, 2, 0):
+    def far_loop(hf, b):
+        def step(n, carry):
+            far_step(n, hf, b)
+            return carry
+
+        lax.fori_loop(0, N_HEAD, step, 0)
+
+    for cp in f_cps[0]:
+        cp.wait()
+    far_loop(1, 0)
+    level_pair(yr, 1, cy, 1, y_cps[1])
+    for cp in f_cps[1]:
+        cp.wait()
+    far_loop(1, 1)
+    for i in PLAN[4]:
         local_chunk(i)
-    lax.fori_loop(N_HEAD, 2 * N_HEAD, far_step, 0)
-
-    ri = lax.broadcasted_iota(jnp.int32, (ROWS, WIN + ROWS), 0)
-    ji = lax.broadcasted_iota(jnp.int32, (ROWS, WIN + ROWS), 1)
-    gap = WIN + ri - ji
-    for b in range(seg // ROWS):
-        reach = jnp.broadcast_to(look[b : b + 1, :].astype(F32), (ROWS, ROWS)).T
-        reach = jnp.concatenate([reach] * 3, axis=1).astype(jnp.int32)
-        key_pos = shard * seg + b * ROWS - WIN + ji
-        ok = (gap >= 0) & (gap <= reach) & (key_pos >= 0)
-        bias[b] = jnp.where(ok, 0.0, -1e30)
-
-    if THROTTLE:
-        for k in (1, 3, 2):
-            z_copy(1, k, to_z(k)).wait_send()
+    far_loop(0, None)
+
     hop = pltpu.make_async_remote_copy(
         src_ref=fen.at[pl.ds(pl.multiple_of(to_z(2) * seg, CHUNK), CHUNK)],
         dst_ref=relay,
@@ -366,8 +366,8 @@
         device_id=at_z(to_z(3)), device_id_type=MESH,
     )
     hop.start()
-    z_copy(0, 1, to_z(1)).start()
-    z_copy(0, 3, to_z(3)).start()
+    z_copy(0, 1, None).start()
+    z_copy(0, 3, None).start()
     onward = pltpu.make_async_remote_copy(
         src_ref=relay,
         dst_ref=xg.at[pl.ds(0, CHUNK), pl.ds(pl.multiple_of(to_z(1) * feat, feat), feat)],
@@ -378,11 +378,22 @@
         src_ref=kvb.at[pl.ds(seg, WIN)], dst_ref=kvb.at[pl.ds(0, WIN)],
         send_sem=h_ss.at[0], recv_sem=h_rs.at[0], device_id=next_dev, device_id_type=MESH,
     )
+    ri = lax.broadcasted_iota(jnp.int32, (ROWS, WIN + ROWS), 0)
+    ji = lax.broadcasted_iota(jnp.int32, (ROWS, WIN + ROWS), 1)
+    gap = WIN + ri - ji
+    for b in range(seg // ROWS):
+        reach = jnp.broadcast_to(look[b : b + 1, :].astype(F32), (ROWS, ROWS)).T
+        reach = jnp.concatenate([reach] * 3, axis=1).astype(jnp.int32)
+        key_pos = shard * seg + b * ROWS - WIN + ji
+        ok = (gap >= 0) & (gap <= reach) & (key_pos >= 0)
+        bias[b] = jnp.where(ok, 0.0, -1e30)
+
     for cp in w_in:
         cp.wait()
 
-    for k in (1, 3, 2):
-        z_copy(1, k, to_z(k)).wait_recv()
+    for b in range(2):
+        for k in (1, 3, 2):
+            z_copy(1, k, b).wait_recv()
     late = slice(CHUNK, 2 * CHUNK)
     for n in range(2):
         wcols = slice(d_model + n * kvd, d_model + (n + 1) * kvd)
@@ -406,7 +417,7 @@
             total = term if total is None else total + term
         return total
 
-    z_copy(0, 1, to_z(1)).wait_recv()
+    z_copy(0, 1, None).wait_recv()
 
     def part_step(n, carry):
         off = pl.ds(pl.multiple_of(n * kvd, kvd), kvd)
@@ -414,7 +425,7 @@
         return carry
 
     lax.fori_loop(0, d_model // kvd + 2, part_step, 0)
-    z_copy(0, 3, to_z(3)).wait_recv()
+    z_copy(0, 3, None).wait_recv()
     onward.wait_recv()
     for n in range(2):
         wcols = pl.ds(d_model + n * kvd, kvd)
@@ -428,14 +439,13 @@
     lax.fori_loop(0, d_model // kvd, q_rest, 0)
 
     halo.wait_recv()
-    core_cp.wait_send()
-    for cp in x_cps + y_cps:
+    for cp in core_cps + x_cps[0] + x_cps[1] + y_cps[0] + y_cps[1]:
         cp.wait_send()
-    if not THROTTLE:
+    for b in range(2):
         for k in (1, 3, 2):
-            z_copy(1, k, to_z(k)).wait_send()
-    z_copy(0, 1, to_z(1)).wait_send()
-    z_copy(0, 3, to_z(3)).wait_send()
+            z_copy(1, k, b).wait_send()
+    z_copy(0, 1, None).wait_send()
+    z_copy(0, 3, None).wait_send()
     hop.wait_send()
     onward.wait_send()
     halo.wait_send()
@@ -516,16 +526,16 @@
             pltpu.VMEM((feat, HD), F32),
             pltpu.VMEM((feat, HD), BF),
             pltpu.VMEM((feat, HD), BF),
-            pltpu.VMEM((SIDE, feat // 2, HD), BF),
-            pltpu.VMEM((SIDE, feat // 2, HD), BF),
+            pltpu.VMEM((2, SIDE, HD, HD), BF),
+            pltpu.VMEM((2, SIDE, HD, HD), BF),
             pltpu.VMEM((feat, FAR * HD), BF),
             pltpu.VMEM((seg, d_model), BF),
             pltpu.VMEM((d_model, d_model + 2 * kvd), BF),
             pltpu.VMEM((CHUNK, feat), BF),
             pltpu.VMEM((CHUNK, d_model + 2 * kvd), F32),
             dma((5, 2)), dma((3,)), dma((4,)),
-            dma((1,)), dma((1,)), dma((SIDE,)), dma((SIDE,)), dma((SIDE,)), dma((SIDE,)),
-            dma((2,)), dma((2,)), dma((2, N_HEAD)), dma((2, N_HEAD)), dma((1,)), dma((1,)),
+            dma((2,)), dma((2,)), dma((2, SIDE)), dma((2, SIDE)), dma((2, SIDE)), dma((2, SIDE)),
+            dma((2, 2)), dma((2, 2)), dma((3, N_HEAD)), dma((3, N_HEAD)), dma((1,)), dma((1,)),
             dma((1,)), dma((1,)),
         ],
         compiler_params=pltpu.CompilerParams(

time: 62.4 us -> 59.4 us (0.952)
  Pallas kernels: 61.4 us -> 58.5 us
    pallas_call x1, Pallas kernels: 55.4 us -> 52.5 us  [shards(): pl.pallas_call(body, out_shape=(pltpu.VMEM((tok, feat), BF), pltpu.VMEM((...]
where the time goes in v3:
time: 59.4 us; the launch traced here: 59.3 us
  Pallas kernels  58.5 us (98%)
  between operations  0.8 us (1%)
    pallas_call x1, Pallas kernels, shards(): pl.pallas_call(body, out_shape=(pltpu.VMEM((tok, feat), BF), pltpu.VMEM((...  52.5 us
    pallas_call x1, Pallas kernels, shards(): pl.pallas_call(attention, out_shape=(jax.ShapeDtypeStruct((tok, feat), BF...  6.02 us

profile of v3, /device:TPU:1, one launch (start us, length us, event | category | flops | bytes accessed | tf_op | source)
XLA Modules:
  0.0 59.3 jit_solution(15631033430868231432)
XLA Ops:
  0.6 52.5 %shard_map.113 = (bf16[2048,512]{1,0:T(8,128)(2,1)S(1)}, bf16[512,2048]{1,0:T(8,128)(2,1)S(1)}, bf16[768,1024]{1,0:T(8,128)(2,1)S(1)}, f32[4,128,384]{2,1,0:T(8,128)S(1)}) custom-call(bf16[2048,512]{1,0:T(8,128)(2,1)} %q_hbm.1, bf16[2048,512]{1,0:T(8,128)(2,1)} %k_hbm.1, bf16[2048,512]{1,0:T(8,128)(2,1)} %v_hbm.1, s32[21,2048]{1,0:T(8,128)} %bitcast.3, ...), custom_call_target="tpu_custom_call" | custom-call | tf_op jit(solution)/shard_map/pallas_call | solution.py:500
  53.1 6.0 %shard_map.114 = (bf16[2048,512]{1,0:T(8,128)(2,1)}, bf16[512,2048]{1,0:T(8,128)(2,1)}) custom-call(bf16[2048,512]{1,0:T(8,128)(2,1)S(1)} %get-tuple-element.6.fen, bf16[512,2048]{1,0:T(8,128)(2,1)S(1)} %get-tuple-element.7.qs, bf16[768,1024]{1,0:T(8,128)(2,1)S(1)} %get-tuple-element.8.kvb, f32[4,128,384]{2,1,0:T(8,128)S(1)} %get-tuple-element.9.bias), custom_call_target="tpu_custom_call" | custom-call | tf_op jit(solution)/shard_map/pallas_call | solution.py:548

commit v4 on v3

--- a/solution.py
+++ b/solution.py
@@ -25,7 +25,7 @@
 BF = jnp.bfloat16
 F32 = jnp.float32
 SCALE = HD ** (-0.5)
-PLAN = ((7,), (5,), (3,), (1,), (6, 4, 2, 0))
+PLAN = ((7,), (5,), (3,), (1,))
 LOG2E = 1.4426950408889634
 
 
@@ -210,9 +210,13 @@
 
     lax.fori_loop(0, chunks, q_step, 0)
 
+    def m(cond):
+        return jnp.where(cond, 1.0, 0.0).astype(F32)
+
     def local_chunk(i):
-        t0 = i * CHUNK
-        cols = slice(t0, t0 + CHUNK)
+        fixed = isinstance(i, int)
+        t0 = i * CHUNK if fixed else pl.multiple_of(i * CHUNK, CHUNK)
+        cols = pl.ds(t0, CHUNK)
 
         def head(h, carry):
             hoff = pl.multiple_of(h * HD, HD)
@@ -223,36 +227,39 @@
 
             def quad(a):
                 lo = t0 + a * HALF
+                lo = lo if fixed else pl.multiple_of(lo, HALF)
                 w = jnp.zeros((HALF, HALF), F32)
                 lv = lev[...]
                 for l in range(NEAR_BITS):
-                    w = jnp.where(lv == l, lamh[l : l + 1, lo : lo + HALF], w)
+                    w = jnp.where(lv == l, lamh[l : l + 1, pl.ds(lo, HALF)], w)
                 return (st[a * HALF : (a + 1) * HALF, a * HALF : (a + 1) * HALF] * w).astype(BF)
 
             cross = (
-                st[:HALF, HALF:] * lamh[NEAR_BITS : NEAR_BITS + 1, t0 + HALF : t0 + CHUNK]
+                st[:HALF, HALF:] * lamh[NEAR_BITS : NEAR_BITS + 1, pl.ds(t0 + HALF if fixed else pl.multiple_of(t0 + HALF, HALF), HALF)]
             ).astype(BF)
             top = jnp.concatenate([quad(0), cross], axis=1)
             low = jnp.concatenate([jnp.zeros((HALF, HALF), BF), quad(1)], axis=1)
             terms = jnp.concatenate([top, low], axis=0)
             acc = mm(vt[hrows, cols], terms)
             used = []
-            if i & 1:
-                used.append((i // 2, 9))
-            if i & 2:
-                used.append((4 + i // 4, 10))
-            if i & 4:
-                used.append((6, 11))
-            for slot, l in used:
-                ql = qth * jnp.broadcast_to(lamh[l : l + 1, cols], (HD, CHUNK)).astype(BF)
-                acc = acc + mm(lst[slot, hrows, :], ql)
+            if fixed:
+                if i & 1:
+                    used.append((i // 2, 9, None))
+                if i & 2:
+                    used.append((4 + i // 4, 10, None))
+                if i & 4:
+                    used.append((6, 11, None))
+            else:
+                used.append((4 + i // 4, 10, m(lax.rem(i // 2, 2) == 1)))
+                used.append((6, 11, m(i >= 4)))
+            for slot, l, keep in used:
+                row = lamh[l : l + 1, cols]
+                row = row if keep is None else row * keep
+                acc = acc + mm(lst[slot, hrows, :], qth * jnp.broadcast_to(row, (HD, CHUNK)).astype(BF))
             loc[hrows, cols] = acc
             return carry
 
         lax.fori_loop(0, HERE, head, 0, unroll=2)
-
-    def m(cond):
-        return jnp.where(cond, 1.0, 0.0).astype(F32)
 
     def level_pair(buf, b, pos, n, cps):
         for cp in cps:
@@ -355,9 +362,6 @@
     for cp in f_cps[1]:
         cp.wait()
     far_loop(1, 1)
-    for i in PLAN[4]:
-        local_chunk(i)
-    far_loop(0, None)
 
     hop = pltpu.make_async_remote_copy(
         src_ref=fen.at[pl.ds(pl.multiple_of(to_z(2) * seg, CHUNK), CHUNK)],
@@ -365,9 +369,23 @@
         send_sem=r_ss.at[0], recv_sem=r_rs.at[0],
         device_id=at_z(to_z(3)), device_id_type=MESH,
     )
-    hop.start()
-    z_copy(0, 1, None).start()
-    z_copy(0, 3, None).start()
+
+    def first_half(n, carry):
+        k = jnp.where(n == 0, 2, jnp.where(n == 1, 1, jnp.where(n == 2, 3, 0)))
+        local_chunk(2 * to_z(k))
+        far_step(n, 0, None)
+
+        @pl.when(n == 0)
+        def _():
+            hop.start()
+
+        @pl.when((n == 1) | (n == 2))
+        def _():
+            z_copy(0, k, None).start()
+
+        return carry
+
+    lax.fori_loop(0, N_HEAD, first_half, 0)
     onward = pltpu.make_async_remote_copy(
         src_ref=relay,
         dst_ref=xg.at[pl.ds(0, CHUNK), pl.ds(pl.multiple_of(to_z(1) * feat, feat), feat)],
@@ -399,6 +417,8 @@
         wcols = slice(d_model + n * kvd, d_model + (n + 1) * kvd)
         kvb[WIN + CHUNK :, n * kvd : (n + 1) * kvd] = mm(xg[late, :], w_v[:, wcols]).astype(BF)
     halo.start()
+    hop.wait_recv()
+    onward.start()
 
     def q_proj(n, carry):
         off = pl.ds(pl.multiple_of(n * kvd, kvd), kvd)
@@ -406,8 +426,6 @@
         return carry
 
     lax.fori_loop(0, d_model // kvd, q_proj, 0)
-    hop.wait_recv()
-    onward.start()
 
     def two(j, k, off):
         total = None

time: 59.4 us -> 59.1 us (level)
  no operation moved by 1% of the time
where the time goes in v4:
time: 59.1 us; the launch traced here: 59 us
  Pallas kernels  58.3 us (99%)
  between operations  0.64 us (1%)
    pallas_call x1, Pallas kernels, shards(): pl.pallas_call(body, out_shape=(pltpu.VMEM((tok, feat), BF), pltpu.VMEM((...  52.3 us
    pallas_call x1, Pallas kernels, shards(): pl.pallas_call(attention, out_shape=(jax.ShapeDtypeStruct((tok, feat), BF...  6.02 us

profile of v4, /device:TPU:1, one launch (start us, length us, event | category | flops | bytes accessed | tf_op | source)
XLA Modules:
  0.0 59.0 jit_solution(17429629425192292343)
XLA Ops:
  0.6 52.3 %shard_map.113 = (bf16[2048,512]{1,0:T(8,128)(2,1)S(1)}, bf16[512,2048]{1,0:T(8,128)(2,1)S(1)}, bf16[768,1024]{1,0:T(8,128)(2,1)S(1)}, f32[4,128,384]{2,1,0:T(8,128)S(1)}) custom-call(bf16[2048,512]{1,0:T(8,128)(2,1)} %q_hbm.1, bf16[2048,512]{1,0:T(8,128)(2,1)} %k_hbm.1, bf16[2048,512]{1,0:T(8,128)(2,1)} %v_hbm.1, s32[21,2048]{1,0:T(8,128)} %bitcast.3, ...), custom_call_target="tpu_custom_call" | custom-call | tf_op jit(solution)/shard_map/pallas_call | solution.py:518
  52.9 6.0 %shard_map.114 = (bf16[2048,512]{1,0:T(8,128)(2,1)}, bf16[512,2048]{1,0:T(8,128)(2,1)}) custom-call(bf16[2048,512]{1,0:T(8,128)(2,1)S(1)} %get-tuple-element.6.fen, bf16[512,2048]{1,0:T(8,128)(2,1)S(1)} %get-tuple-element.7.qs, bf16[768,1024]{1,0:T(8,128)(2,1)S(1)} %get-tuple-element.8.kvb, f32[4,128,384]{2,1,0:T(8,128)S(1)} %get-tuple-element.9.bias), custom_call_target="tpu_custom_call" | custom-call | tf_op jit(solution)/shard_map/pallas_call | solution.py:566

commit v5 on v4

--- a/solution.py
+++ b/solution.py
@@ -119,7 +119,7 @@
                     cst[i, hs, :] = mm(vtc, k_v[rows, hs])
                 return carry
 
-            lax.fori_loop(n * chunks // 4, (n + 1) * chunks // 4, state_step, 0)
+            lax.fori_loop(n * chunks // 4, (n + 1) * chunks // 4, state_step, 0, unroll=2)
         hs = slice(2 * b * HD, (2 * b + 2) * HD)
         pairs = [cst[2 * j, hs, :] + cst[2 * j + 1, hs, :] for j in range(4)]
         lo4 = pairs[0] + pairs[1]
@@ -492,12 +492,13 @@
 
     copies = [fen_out]
     for b in range(qs.shape[0] // ROWS):
+        rows = pl.ds(b * ROWS, ROWS)
         for g in range(KV_HEADS):
             attend(b, g)
-        rows = pl.ds(b * ROWS, ROWS)
-        cp = pltpu.make_async_copy(att.at[rows], att_hbm.at[rows], out_sem.at[1 + b])
-        cp.start()
-        copies.append(cp)
+            piece = (rows, pl.ds(g * GROUPS * HD, GROUPS * HD))
+            cp = pltpu.make_async_copy(att.at[piece], att_hbm.at[piece], out_sem.at[1 + b * KV_HEADS + g])
+            cp.start()
+            copies.append(cp)
     for cp in copies:
         cp.wait()
 
@@ -571,7 +572,7 @@
         ),
         in_specs=[vmem] * 4,
         out_specs=(hbm, hbm),
-        scratch_shapes=[pltpu.VMEM((seg, d_model), BF), dma((1 + seg // ROWS,))],
+        scratch_shapes=[pltpu.VMEM((seg, d_model), BF), dma((1 + seg // ROWS * KV_HEADS,))],
         compiler_params=pltpu.CompilerParams(vmem_limit_bytes=32 << 20),
     )(*mid)
 

time: 59.1 us -> 58.3 us (0.986)
  Pallas kernels: 58.3 us -> 57.6 us
    pallas_call x1, Pallas kernels: 52.3 us -> 51.6 us  [shards(): pl.pallas_call(body, out_shape=(pltpu.VMEM((tok, feat), BF), pltpu.VMEM((...]
where the time goes in v5:
time: 58.3 us; the launch traced here: 58.2 us
  Pallas kernels  57.6 us (99%)
  between operations  0.64 us (1%)
    pallas_call x1, Pallas kernels, shards(): pl.pallas_call(body, out_shape=(pltpu.VMEM((tok, feat), BF), pltpu.VMEM((...  51.6 us
    pallas_call x1, Pallas kernels, shards(): pl.pallas_call(attention, out_shape=(jax.ShapeDtypeStruct((tok, feat), BF...  5.98 us

profile of v5, /device:TPU:1, one launch (start us, length us, event | category | flops | bytes accessed | tf_op | source)
XLA Modules:
  0.0 58.2 jit_solution(16563592386820835263)
XLA Ops:
  0.6 51.6 %shard_map.113 = (bf16[2048,512]{1,0:T(8,128)(2,1)S(1)}, bf16[512,2048]{1,0:T(8,128)(2,1)S(1)}, bf16[768,1024]{1,0:T(8,128)(2,1)S(1)}, f32[4,128,384]{2,1,0:T(8,128)S(1)}) custom-call(bf16[2048,512]{1,0:T(8,128)(2,1)} %q_hbm.1, bf16[2048,512]{1,0:T(8,128)(2,1)} %k_hbm.1, bf16[2048,512]{1,0:T(8,128)(2,1)} %v_hbm.1, s32[21,2048]{1,0:T(8,128)} %bitcast.3, ...), custom_call_target="tpu_custom_call" | custom-call | tf_op jit(solution)/shard_map/pallas_call | solution.py:519
  52.3 6.0 %shard_map.114 = (bf16[2048,512]{1,0:T(8,128)(2,1)}, bf16[512,2048]{1,0:T(8,128)(2,1)}) custom-call(bf16[2048,512]{1,0:T(8,128)(2,1)S(1)} %get-tuple-element.6.fen, bf16[512,2048]{1,0:T(8,128)(2,1)S(1)} %get-tuple-element.7.qs, bf16[768,1024]{1,0:T(8,128)(2,1)S(1)} %get-tuple-element.8.kvb, f32[4,128,384]{2,1,0:T(8,128)S(1)} %get-tuple-element.9.bias), custom_call_target="tpu_custom_call" | custom-call | tf_op jit(solution)/shard_map/pallas_call | solution.py:567
